TPU v7x, 32 devices: a whole 2x2x4 slice. The times are simulated.
32 devices in a mesh: ctx: 2 (over x), head: 4 (over y, core), rep: 4 (over z).
Axes of the slice: x: 2, y: 2, z: 4, core: 2. Of those that a mesh axis runs over, the one named last changes fastest.
Arguments:
- kv_cache: float32 [8, 2, 512, 8, 128], P('head', None, 'ctx', 'rep'), may hold values from -8 to 8
- prefill_q: float32 [8, 256, 64, 128], P('head', 'ctx', 'rep'), may hold values from -512 to 512
- decode_q: float32 [8, 8, 4, 64, 128], P(None, ('ctx', 'rep'), None, 'head'), may hold values from -512 to 512
- decode_kv: float32 [8, 8, 4, 2, 8, 128], P(None, ('ctx', 'rep'), None, None, 'head'), may hold values from -12 to 12
- lengths: int32 [8], replicated, may hold values from 256 to 512, as said below
- row_length: int32 [8, 8], P(None, ('ctx', 'rep')), may hold values from 2 to 512, as said below
Outputs:
- prefill_out: float32 [8, 256, 64, 128], P('head', 'ctx', 'rep')
- decode_out: float32 [8, 8, 4, 64, 128], P(None, ('ctx', 'rep'), None, 'head')
Inputs may be any that keep to these rules, and one draw needn't show every extreme that they name: `lengths`: multiples of 128; some request has length 512. `row_length`: a row reads at most its request's length; every request has a row that reads its whole length.
All inputs are finite; a program needn't handle non-finite values.
Results may differ from a plain program's by a relative error of at most 0.0003.
Values sent between devices are 32-bit elements; how exact they have to be, the bound alone decides.
No kernel may reach another device: no remote copies, remote signals or barrier semaphores. Data moves between devices by JAX's collectives and lax.ppermute only.
A program may use at most 128 MiB of HBM per device.

v0:
```python
import math
import jax
import jax.numpy as jnp
from jax import lax
from jax.sharding import PartitionSpec as P

NEG_FILL = -1e30
HIGH_PRECISION = lax.Precision.HIGHEST


def broadcast(value, axis, source):
    kept = jnp.where(lax.axis_index(axis) == source, value, 0).astype(value.dtype)
    return lax.psum(kept, axis)


def online_fold(running, scores, value_rows, pattern):
    run_max, run_total, run_acc = running
    new_max = jnp.maximum(run_max, jnp.max(scores, axis=-1))
    weights = jnp.exp(scores - new_max[..., None])
    new_total = jnp.sum(weights, axis=-1)
    new_acc = jnp.einsum(pattern, weights, value_rows, precision=HIGH_PRECISION)
    return (new_max, new_total, new_acc)


def empty_state(lead_shape, head_dim):
    return (
        jnp.full(lead_shape, NEG_FILL, jnp.float32),
        jnp.zeros(lead_shape, jnp.float32),
        jnp.zeros(lead_shape + (head_dim,), jnp.float32),
    )


def block_fold(running, query_rows, key_block, first_pos, limits, score_scale, strict):
    block_len = key_block.shape[2]
    scores = (
        jnp.einsum("bkrd,bnkd->bkrn", query_rows, key_block[:, 0], precision=HIGH_PRECISION)
        * score_scale
    )
    positions = first_pos + jnp.arange(block_len, dtype=jnp.int32)
    if strict:
        allowed = positions[None, None, :] < limits[:, :, None]
    else:
        allowed = positions[None, None, :] <= limits[:, :, None]
    scores = jnp.where(allowed[:, None], scores, NEG_FILL)
    return online_fold(running, scores, key_block[:, 1], "bkrn,bnkd->bkrd")


def source_major(values, slot_count, kv_heads, sources, count_rows, step_count, group_size):
    tail_shape = values.shape[3:]
    spread_out = values.reshape(
        (slot_count, kv_heads, sources, count_rows, step_count, group_size) + tail_shape
    )
    axes_order = (2, 0, 3, 4, 1, 5) + tuple(range(6, 6 + len(tail_shape)))
    moved = jnp.transpose(spread_out, axes_order)
    return moved.reshape(
        (sources, slot_count, count_rows, step_count, kv_heads * group_size) + tail_shape
    )


def on_device(kv_cache, prefill_q, decode_q, decode_kv, lengths, row_length):
    ctx_count = lax.axis_size("ctx")
    ctx_index = lax.axis_index("ctx")
    head_index = lax.axis_index("head")
    req_group, span_rows, rep_heads, head_dim = prefill_q.shape
    rep_kv = kv_cache.shape[3]
    group_size = rep_heads // rep_kv
    block_len = kv_cache.shape[2]
    score_scale = 1.0 / math.sqrt(head_dim)
    group_lengths = lax.dynamic_slice_in_dim(lengths, head_index * req_group, req_group)
    span_pos = (
        group_lengths[:, None]
        - span_rows * ctx_count
        + ctx_index * span_rows
        + jnp.arange(span_rows, dtype=jnp.int32)[None, :]
    )
    row_pos = jnp.repeat(span_pos, group_size, axis=1)
    prefill_rows = jnp.transpose(
        prefill_q.reshape(req_group, span_rows, rep_kv, group_size, head_dim), (0, 2, 1, 3, 4)
    ).reshape(req_group, rep_kv, span_rows * group_size, head_dim)
    start_state = empty_state((req_group, rep_kv, span_rows * group_size), head_dim)
    run_max, run_total, run_acc = block_fold(
        start_state,
        prefill_rows,
        lax.all_gather(kv_cache, "ctx", axis=2, tiled=True),
        jnp.int32(0),
        row_pos,
        score_scale,
        False,
    )
    prefill_vals = run_acc / run_total[..., None]
    prefill_out = jnp.transpose(
        prefill_vals.reshape(req_group, rep_kv, span_rows, group_size, head_dim), (0, 2, 1, 3, 4)
    ).reshape(prefill_q.shape)
    all_requests = lax.all_gather(kv_cache, "head", axis=0, tiled=True)
    head_cache = broadcast(all_requests, "rep", head_index)
    requests, row_count, step_count, local_heads, unused_dim = decode_q.shape
    kv_heads = local_heads // group_size
    gathered_rows, gathered_limits = (
        lax.all_gather(decode_q, "ctx", axis=1, tiled=True),
        lax.all_gather(row_length, "ctx", axis=1, tiled=True),
    )
    total_rows = gathered_rows.shape[1]
    grouped = jnp.transpose(
        gathered_rows.reshape(requests, total_rows, step_count, kv_heads, group_size, head_dim),
        (0, 3, 1, 2, 4, 5),
    ).reshape(requests, kv_heads, -1, head_dim)
    limits = jnp.broadcast_to(
        gathered_limits[:, :, None, None], (requests, total_rows, step_count, group_size)
    ).reshape(requests, -1)
    running = empty_state((requests, kv_heads, grouped.shape[2]), head_dim)
    running = block_fold(
        running, grouped, head_cache, ctx_index * block_len, limits, score_scale, True
    )
    shaped = tuple(
        (
            source_major(values, requests, kv_heads, ctx_count, row_count, step_count, group_size)
            for values in running
        )
    )
    home_max, home_total, home_acc = (
        lax.all_to_all(shaped[0], "ctx", split_axis=0, concat_axis=0, tiled=True),
        lax.all_to_all(shaped[1], "ctx", split_axis=0, concat_axis=0, tiled=True),
        lax.all_to_all(shaped[2], "ctx", split_axis=0, concat_axis=0, tiled=True),
    )
    ctx_max = jnp.max(home_max, axis=0)
    factor = jnp.exp(home_max - ctx_max[None])
    ctx_total = jnp.sum(home_total * factor, axis=0)
    ctx_acc = jnp.sum(home_acc * factor[..., None], axis=0)
    home_rows = decode_q.reshape(requests, row_count, step_count, kv_heads, group_size, head_dim)
    draft_scores = (
        jnp.einsum(
            "artkgd,arskd->artkgs", home_rows, decode_kv[:, :, :, 0], precision=HIGH_PRECISION
        )
        * score_scale
    )
    step_ids = jnp.arange(step_count, dtype=jnp.int32)
    causal = step_ids[None, :] <= step_ids[:, None]
    draft_scores = jnp.where(causal[None, None, :, None, None, :], draft_scores, NEG_FILL)
    ctx_max = ctx_max.reshape(requests, row_count, step_count, kv_heads, group_size)
    ctx_total = ctx_total.reshape(requests, row_count, step_count, kv_heads, group_size)
    ctx_acc = ctx_acc.reshape(requests, row_count, step_count, kv_heads, group_size, head_dim)
    joint_max = jnp.maximum(ctx_max, jnp.max(draft_scores, axis=-1))
    draft_weights = jnp.exp(draft_scores - joint_max[..., None])
    ctx_factor = jnp.exp(ctx_max - joint_max)
    denominator = ctx_total * ctx_factor + jnp.sum(draft_weights, axis=-1)
    numerator = ctx_acc * ctx_factor[..., None] + jnp.einsum(
        "artkgs,arskd->artkgd", draft_weights, decode_kv[:, :, :, 1], precision=HIGH_PRECISION
    )
    decode_out = (numerator / denominator[..., None]).reshape(decode_q.shape)
    return (prefill_out, decode_out)


def solution(mesh):
    in_specs = (
        P("head", None, "ctx", "rep", None),
        P("head", "ctx", "rep", None),
        P(None, ("ctx", "rep"), None, "head", None),
        P(None, ("ctx", "rep"), None, None, "head", None),
        P(),
        P(None, ("ctx", "rep")),
    )
    out_specs = (P("head", "ctx", "rep", None), P(None, ("ctx", "rep"), None, "head", None))
    return jax.shard_map(
        on_device, mesh=mesh, in_specs=in_specs, out_specs=out_specs, check_vma=False
    )
```

profile of v0, /device:TPU:0, one launch (start us, length us, event | category | flops | bytes accessed | tf_op | source)
XLA Modules:
  0.0 285.3 jit_solution(5755422686790085839)
XLA Ops:
  7.2 2.4 copy.82
  10.5 36.9 %all-gather.6.cloned.1.call-done = f32[8,2,256,2,128]{4,2,3,0,1:T(8,128)} async-done(((f32[2,2,256,2,128]{4,2,3,0,1:T(8,128)}), f32[8,2,256,2,128]{4,2,3,0,1:T(8,128)}) %all-gather.6.cloned.1.call-update) | async-done | bytes 4194320 | tf_op jit(solution)/shard_map/all_gather | solution.py:94
  47.4 4.6 %broadcast_select_fusion = f32[8,2,256,2,128]{4,2,3,0,1:T(8,128)} fusion(f32[8,2,256,2,128]{4,2,3,0,1:T(8,128)} %all-gather.6.cloned.1.call-done, pred[]{:T(512)S(6)} %eq.3), kind=kLoop, calls=%fused_computation.18 | loop fusion | flops 1048576 | bytes 8388609 | tf_op jit(solution)/shard_map/jit(_where)/select_n | solution.py:12
  52.6 4.2 %all-gather = s32[2,1,8]{2,1,0:T(1,128)S(1)} all-gather(s32[1,1,8]{2,1,0:T(1,128)S(1)} %bitcast.147), channel_id=1, replica_groups=mesh['ctx'=2,'head'=4,'rep'=4] {'ctx'}, dimensions={0}, use_global_device_ids=true | all-gather | bytes 96 | tf_op jit(solution)/shard_map/all_gather | solution.py:100
  57.5 12.6 %all_gather.15 = f32[8,2,4,16,128]{4,3,2,1,0:T(8,128)S(1)} all-gather(f32[8,1,4,16,128]{4,3,2,1,0:T(8,128)S(1)} %copy-done.1), channel_id=1, replica_groups=mesh['ctx'=2,'head'=4,'rep'=4] {'ctx'}, dimensions={1}, use_global_device_ids=true | all-gather | bytes 786432 | tf_op jit(solution)/shard_map/all_gather | solution.py:99
  70.0 0.9 copy.87
  71.1 3.6 %fusion.31 = (f32[8,4,2,8]{3,1,2,0:T(4,128)S(1)}, f32[8,1,4,2,8,4]{4,5,2,3,0,1:T(4,128)S(1)}) fusion(f32[8,1,4,1,2,128]{5,4,3,2,1,0:T(2,128)S(1)} %get-tuple-element.13, pred[4,4]{1,0:T(4,128)(4,1)S(1)} %iota_compare_fusion.1, f32[8,1,4,16,128]{4,3,2,1,0:T(8,128)S(1)} %copy-done.1), kind=kOutput, calls=%fused_computation.63 | convolution fusion | flops 3151360 | bytes 305168 | tf_op jit(solution)/shard_map/artkgd,arskd->artkgs/dot_general | solution.py:131
  75.3 10.6 %all-gather.4.cloned.1.call-done = f32[2,2,512,2,128]{4,2,3,0,1:T(8,128)} async-done(((f32[2,2,256,2,128]{4,2,3,0,1:T(8,128)}), f32[2,2,512,2,128]{4,2,3,0,1:T(8,128)}) %all-gather.4.cloned.1.call-update) | async-done | bytes 2097168 | tf_op jit(solution)/shard_map/all_gather | solution.py:84
  86.0 9.6 %fusion = (f32[2,2,1024]{2,1,0:T(2,128)S(1)}, f32[2,2,1024,512]{2,3,1,0:T(8,128)S(1)}) fusion(pred[2,1024,512]{1,2,0:T(8,128)(4,1)S(1)} %iota_compare_fusion, f32[2,2,512,2,128]{4,2,3,0,1:T(8,128)} %all-gather.4.cloned.1.call-done, f32[2,128,16,128]{3,2,1,0:T(8,128)S(1)} %copy-done), kind=kOutput, calls=%fused_computation.2 | convolution fusion | flops 3227512832 | bytes 12599296 | tf_op jit(solution)/shard_map/bkrd,bnkd->bkrn/dot_general | solution.py:36
  95.6 2.2 fusion.1
  97.8 15.4 %divide_bitcast_fusion = f32[2,128,2,8,128]{4,3,1,2,0:T(8,128)S(1)} fusion(f32[2,2,1024]{2,1,0:T(2,128)S(1)} %fusion.1, f32[2,2,512,2,128]{4,2,3,0,1:T(8,128)S(1)} %copy-done.2, f32[2,2,1024,512]{2,3,1,0:T(8,128)S(1)} %get-tuple-element.17, f32[2,2,1024]{2,1,0:T(2,128)S(1)} %broadcast_maximum_fusion, pred[2,1024,512]{1,2,0:T(8,128)(4,1)S(1)} %iota_compare_fusion), kind=kOutput, calls=%fused_computation.19 | convolution fusion | flops 3228041216 | bytes 12615680 | tf_op jit(solution)/shard_map/bkrn,bnkd->bkrd/dot_general | solution.py:21
  113.3 1.5 copy.141
  114.8 130.5 %all-reduce.2.cloned.1.call-done = f32[8,2,256,2,128]{4,2,3,0,1:T(8,128)} async-done(((f32[8,2,256,2,128]{4,2,3,0,1:T(8,128)}), f32[8,2,256,2,128]{4,2,3,0,1:T(8,128)}) %all-reduce.2.cloned.1.call-update) | async-done | bytes 4194320 | tf_op jit(solution)/shard_map/psum | solution.py:13
  245.2 4.1 %fusion.30 = (f32[8,2,64]{2,1,0:T(2,128)S(1)}, f32[8,2,64,256]{3,2,1,0:T(8,128)S(1)}) fusion(f32[8,2,64,128]{3,2,1,0:T(8,128)} %bitcast.142, f32[8,2,256,2,128]{4,2,3,0,1:T(8,128)} %all-reduce.2.cloned.1.call-done, pred[8,64,256]{2,1,0:T(8,128)(4,1)S(1)} %broadcast_compare_fusion), kind=kOutput, calls=%fused_computation.62 | convolution fusion | flops 403438592 | bytes 3805184 | tf_op jit(solution)/shard_map/bkrd,bnkd->bkrn/dot_general | solution.py:36
  250.8 3.2 %all-to-all-start.2 = ((f32[2,1,512]{2,1,0:T(1,128)}), f32[2,1,512]{2,1,0:T(1,128)S(1)}, u32[]{:S(2)}, u32[]{:S(2)}) async-start(f32[2,1,512]{2,1,0:T(1,128)} %reshape.235), calls=%async_computation.2 | async-start | bytes 8192 | tf_op jit(solution)/shard_map/all_to_all | solution.py:122
  255.0 2.8 all-to-all-done.2
  257.8 3.2 %all-to-all-start.1 = ((f32[2,1,512]{2,1,0:T(1,128)}), f32[2,1,512]{2,1,0:T(1,128)S(1)}, u32[]{:S(2)}, u32[]{:S(2)}) async-start(f32[2,1,512]{2,1,0:T(1,128)} %reshape.233), calls=%async_computation.1 | async-start | bytes 8192 | tf_op jit(solution)/shard_map/all_to_all | solution.py:121
  261.0 3.3 %fusion.7 = f32[8,2,64,128]{3,2,1,0:T(8,128)S(1)} fusion(f32[8,2,256,2,128]{4,2,3,0,1:T(8,128)} %all-reduce.2.cloned.1.call-done, f32[8,2,64,256]{3,2,1,0:T(8,128)S(1)} %get-tuple-element.19, f32[8,2,64]{2,1,0:T(2,128)S(1)} %broadcast_maximum_fusion.1), kind=kOutput, calls=%fused_computation.11 | convolution fusion | flops 402915328 | bytes 3674112 | tf_op jit(solution)/shard_map/bkrn,bnkd->bkrd/dot_general | solution.py:21
  264.3 0.8 copy.142
  265.8 0.7 reduce.6
  266.6 3.5 %all-to-all-start = ((f32[2,8,1,4,16,128]{5,4,3,1,2,0:T(8,128)}), f32[2,8,1,4,16,128]{5,4,3,1,2,0:T(8,128)S(1)}, u32[]{:S(2)}, u32[]{:S(2)}) async-start(f32[2,8,1,4,16,128]{5,4,3,1,2,0:T(8,128)} %bitcast.137), calls=%async_computation | async-start | bytes 1048576 | tf_op jit(solution)/shard_map/all_to_all | solution.py:123
  270.1 0.7 reduce.5
  271.3 5.9 %all-to-all-done = f32[2,8,1,4,16,128]{5,4,3,1,2,0:T(8,128)S(1)} async-done(((f32[2,8,1,4,16,128]{5,4,3,1,2,0:T(8,128)}), f32[2,8,1,4,16,128]{5,4,3,1,2,0:T(8,128)S(1)}, u32[]{:S(2)}, u32[]{:S(2)}) %all-to-all-start) | async-done | bytes 524320 | tf_op jit(solution)/shard_map/all_to_all | solution.py:123
  278.0 0.7 copy.143
  (59 shorter events, 7.2 us)
Async XLA Ops:
  7.2 78.8 %copy-start = (f32[2,128,16,128]{3,2,1,0:T(8,128)S(1)}, f32[2,128,16,128]{3,2,1,0:T(8,128)}, u32[]{:S(2)}) copy-start(f32[2,128,16,128]{3,2,1,0:T(8,128)} %param.7) | copy-start | bytes 6291460
  7.2 40.2 %all-gather.6.cloned.1.call-start = ((), (), s32[]{:S(2)}) async-start(), calls=%async_computation.4 | async-start | bytes 5242880 | tf_op jit(solution)/shard_map/all_gather | solution.py:94
  9.7 76.3 %all-gather.4.cloned.1.call-start = ((), (), s32[]{:S(2)}) async-start(), calls=%async_computation.3 | async-start | bytes 3145728 | tf_op jit(solution)/shard_map/all_gather | solution.py:84
  10.4 234.8 %all-reduce.2.cloned.1.call-start = ((), (), s32[]{:S(2)}) async-start(), calls=%async_computation.5 | async-start | bytes 8388608 | tf_op jit(solution)/shard_map/psum | solution.py:13
  52.0 0.7 copy-start.5
  52.0 5.1 %copy-start.4 = (s32[8]{0:T(128)S(1)}, s32[8]{0:T(128)}, u32[]{:S(2)}) copy-start(s32[8]{0:T(128)} %param.10) | copy-start | bytes 100
  52.0 5.5 %copy-start.1 = (f32[8,1,4,16,128]{4,3,2,1,0:T(8,128)S(1)}, f32[8,1,4,16,128]{4,3,2,1,0:T(8,128)}, u32[]{:S(2)}) copy-start(f32[8,1,4,16,128]{4,3,2,1,0:T(8,128)} %param.8) | copy-start | bytes 786436
  52.0 19.0 %copy-start.3 = (f32[8,1,4,2,2,128]{5,4,3,2,1,0:T(2,128)S(1)}, f32[8,1,4,2,2,128]{5,4,3,2,1,0:T(2,128)}, u32[]{:S(2)}) copy-start(f32[8,1,4,2,2,128]{5,4,3,2,1,0:T(2,128)} %param.9) | copy-start | bytes 196612
  95.6 2.2 copy-start.2
  250.8 7.0 %all-to-all-start.2 = ((f32[2,1,512]{2,1,0:T(1,128)}), f32[2,1,512]{2,1,0:T(1,128)S(1)}, u32[]{:S(2)}, u32[]{:S(2)}) async-start(f32[2,1,512]{2,1,0:T(1,128)} %reshape.235), calls=%async_computation.2 | async-start | bytes 8192 | tf_op jit(solution)/shard_map/all_to_all | solution.py:122
  257.8 8.8 %all-to-all-start.1 = ((f32[2,1,512]{2,1,0:T(1,128)}), f32[2,1,512]{2,1,0:T(1,128)S(1)}, u32[]{:S(2)}, u32[]{:S(2)}) async-start(f32[2,1,512]{2,1,0:T(1,128)} %reshape.233), calls=%async_computation.1 | async-start | bytes 8192 | tf_op jit(solution)/shard_map/all_to_all | solution.py:121
  266.6 10.6 %all-to-all-start = ((f32[2,8,1,4,16,128]{5,4,3,1,2,0:T(8,128)}), f32[2,8,1,4,16,128]{5,4,3,1,2,0:T(8,128)S(1)}, u32[]{:S(2)}, u32[]{:S(2)}) async-start(f32[2,8,1,4,16,128]{5,4,3,1,2,0:T(8,128)} %bitcast.137), calls=%async_computation | async-start | bytes 1048576 | tf_op jit(solution)/shard_map/all_to_all | solution.py:123
Sparse Core Ops, SparseCore 0:
  10.2 37.1 all-gather.5
  49.5 36.4 all-gather.3
  88.4 156.8 all-reduce.1
where the time goes:
time: 286 us; the launch traced here: 285 us
  waiting for transfers between devices  187 us (65%)
  matrix products  36.7 us (13%)
  blocking collectives  16.8 us (6%)
  between operations  14 us (5%)
  local copies, waits for them, and re-layouts  10.3 us (4%)
  starting transfers between devices  10 us (3%)
  other arithmetic  10 us (3%)
    psum x1, waiting for transfers between devices, broadcast(): return lax.psum(kept, axis)  130 us
    all_gather x1, waiting for transfers between devices, on_device(): all_requests = lax.all_gather(kv_cache, 'head', axis=0, tiled=True)  36.9 us
    dot_general x2, matrix products, online_fold(): new_acc = jnp.einsum(pattern, weights, value_rows, precision=HIGH_PRECISION)  18.8 us
    dot_general x2, matrix products, block_fold(): jnp.einsum('bkrd,bnkd->bkrn', query_rows, key_block[:, 0], precision=HIGH...  13.7 us
    all_gather x1, blocking collectives, on_device(): lax.all_gather(decode_q, 'ctx', axis=1, tiled=True)  12.6 us
    all_gather x1, waiting for transfers between devices, on_device(): lax.all_gather(kv_cache, 'ctx', axis=2, tiled=True)  10.6 us
    all_to_all x1, waiting for transfers between devices, on_device(): lax.all_to_all(shaped[2], 'ctx', split_axis=0, concat_axis=0, tiled=True)  5.85 us
  transfers between devices with their start and end apart: 6, of which 5 were waited for; matrix products, arithmetic and copies ran while one was open for 16% of the time, Pallas kernels for 0%

commit v1 on v0

--- a/solution.py
+++ b/solution.py
@@ -91,7 +91,14 @@
     prefill_out = jnp.transpose(
         prefill_vals.reshape(req_group, rep_kv, span_rows, group_size, head_dim), (0, 2, 1, 3, 4)
     ).reshape(prefill_q.shape)
-    all_requests = lax.all_gather(kv_cache, "head", axis=0, tiled=True)
+    size = lax.axis_size("head")
+    right = [(i, (i + 1) % size) for i in range(size)]
+    parts = [kv_cache]
+    for hop in range(1, size):
+        parts = [lax.ppermute(parts[0], "head", right), *parts]
+    whole = jnp.concatenate(parts, axis=0)
+    places = (lax.axis_index("head") + 1) * parts[-1].shape[0]
+    all_requests = jnp.roll(whole, places, axis=0)
     head_cache = broadcast(all_requests, "rep", head_index)
     requests, row_count, step_count, local_heads, unused_dim = decode_q.shape
     kv_heads = local_heads // group_size

time: 286 us -> 264 us (0.923)
  waiting for transfers between devices: 187 us -> 155 us
  local copies, waits for them, and re-layouts: 10.3 us -> 18 us
    ppermute x0 -> x3, waiting for transfers between devices: none -> 43.4 us  [on_device(): parts = [lax.ppermute(parts[0], 'head', right), *parts]]
    all_gather x1 -> x0, waiting for transfers between devices: 36.9 us -> none  [on_device(): all_requests = lax.all_gather(kv_cache, 'head', axis=0, tiled=True)]
    psum x1, waiting for transfers between devices: 130 us -> 103 us  [broadcast(): return lax.psum(kept, axis)]
    all_gather x1, waiting for transfers between devices: 10.6 us -> 0.02 us  [on_device(): lax.all_gather(kv_cache, 'ctx', axis=2, tiled=True)]
    unnamed x20 -> x37, local copies, waits for them, and re-layouts: 4.68 us -> 11.7 us
  transfers between devices with their start and end apart: 6 -> 8, of which waited for: 5 -> 6; matrix products, arithmetic and copies ran while one was open for 16% -> 20% of each run, Pallas kernels for 0% -> 0%
where the time goes in v1:
time: 264 us; the launch traced here: 263 us
  waiting for transfers between devices  155 us (59%)
  matrix products  38.2 us (14%)
  local copies, waits for them, and re-layouts  18 us (7%)
  blocking collectives  17.1 us (6%)
  between operations  15.9 us (6%)
  starting transfers between devices  10.5 us (4%)
  other arithmetic  8.33 us (3%)
    psum x1, waiting for transfers between devices, broadcast(): return lax.psum(kept, axis)  103 us
    ppermute x3, waiting for transfers between devices, on_device(): parts = [lax.ppermute(parts[0], 'head', right), *parts]  43.4 us
    dot_general x2, matrix products, online_fold(): new_acc = jnp.einsum(pattern, weights, value_rows, precision=HIGH_PRECISION)  18.7 us
    dot_general x2, matrix products, block_fold(): jnp.einsum('bkrd,bnkd->bkrn', query_rows, key_block[:, 0], precision=HIGH...  13.9 us
    all_gather x1, blocking collectives, on_device(): lax.all_gather(decode_q, 'ctx', axis=1, tiled=True)  12.7 us
    unnamed x37, local copies, waits for them, and re-layouts  11.7 us
    all_to_all x1, waiting for transfers between devices, on_device(): lax.all_to_all(shaped[2], 'ctx', split_axis=0, concat_axis=0, tiled=True)  5.74 us
  transfers between devices with their start and end apart: 8, of which 6 were waited for; matrix products, arithmetic and copies ran while one was open for 20% of the time, Pallas kernels for 0%

profile of v1, /device:TPU:0, one launch (start us, length us, event | category | flops | bytes accessed | tf_op | source)
XLA Modules:
  0.0 263.1 jit_solution(4128421607211375304)
XLA Ops:
  8.1 2.5 copy.90
  11.0 14.6 %collective-permute-done = f32[2,2,256,2,128]{4,2,3,0,1:T(8,128)S(1)} collective-permute-done((f32[2,2,256,2,128]{4,2,3,0,1:T(8,128)}, f32[2,2,256,2,128]{4,2,3,0,1:T(8,128)S(1)}, u32[]{:S(2)}, u32[]{:S(2)}) %collective-permute-start) | collective-permute-done | bytes 1048608 | tf_op jit(solution)/shard_map/ppermute | solution.py:98
  26.7 14.3 %collective-permute-done.1 = f32[2,2,256,2,128]{4,2,3,0,1:T(8,128)} collective-permute-done((f32[2,2,256,2,128]{4,2,3,0,1:T(8,128)S(1)}, f32[2,2,256,2,128]{4,2,3,0,1:T(8,128)}, u32[]{:S(2)}, u32[]{:S(2)}) %collective-permute-start.1) | collective-permute-done | bytes 1048608 | tf_op jit(solution)/shard_map/ppermute | solution.py:98
  41.1 14.4 %collective-permute-done.2 = f32[2,2,256,2,128]{4,2,3,0,1:T(8,128)} collective-permute-done((f32[2,2,256,2,128]{4,2,3,0,1:T(8,128)}, f32[2,2,256,2,128]{4,2,3,0,1:T(8,128)}, u32[]{:S(2)}, u32[]{:S(2)}) %collective-permute-start.2) | collective-permute-done | bytes 1048608 | tf_op jit(solution)/shard_map/ppermute | solution.py:98
  56.8 1.3 constant_dynamic-update-slice_fusion.6
  58.1 1.3 constant_dynamic-update-slice_fusion.5
  59.5 1.3 constant_dynamic-update-slice_fusion.3
  62.3 2.3 dynamic-slice_select_fusion
  64.6 4.4 %all-gather = s32[2,1,8]{2,1,0:T(1,128)S(1)} all-gather(s32[1,1,8]{2,1,0:T(1,128)S(1)} %bitcast.147), channel_id=1, replica_groups=mesh['ctx'=2,'head'=4,'rep'=4] {'ctx'}, dimensions={0}, use_global_device_ids=true | all-gather | bytes 96 | tf_op jit(solution)/shard_map/all_gather | solution.py:107
  69.3 12.7 %all_gather.11 = f32[8,2,4,16,128]{4,3,2,1,0:T(8,128)S(1)} all-gather(f32[8,1,4,16,128]{4,3,2,1,0:T(8,128)S(1)} %copy-done.4), channel_id=1, replica_groups=mesh['ctx'=2,'head'=4,'rep'=4] {'ctx'}, dimensions={1}, use_global_device_ids=true | all-gather | bytes 786432 | tf_op jit(solution)/shard_map/all_gather | solution.py:106
  84.7 4.2 %fusion.31 = (f32[8,4,2,8]{3,1,2,0:T(4,128)}, f32[8,1,4,2,8,4]{4,5,2,3,0,1:T(4,128)S(1)}) fusion(f32[8,1,4,1,2,128]{5,4,3,2,1,0:T(2,128)S(1)} %get-tuple-element.13, pred[4,4]{1,0:T(4,128)(4,1)S(1)} %iota_compare_fusion.1, f32[8,1,4,16,128]{4,3,2,1,0:T(8,128)S(1)} %copy-done.4), kind=kOutput, calls=%fused_computation.71 | convolution fusion | flops 3151360 | bytes 305168 | tf_op jit(solution)/shard_map/artkgd,arskd->artkgs/dot_general | solution.py:138
  89.6 9.7 %fusion = (f32[2,2,1024]{2,1,0:T(2,128)S(1)}, f32[2,2,1024,512]{2,3,1,0:T(8,128)S(1)}) fusion(pred[2,1024,512]{1,2,0:T(8,128)(4,1)S(1)} %iota_compare_fusion, f32[2,2,512,2,128]{4,2,3,0,1:T(8,128)} %all-gather.3.cloned.1.call-done, f32[2,128,16,128]{3,2,1,0:T(8,128)S(1)} %copy-done), kind=kOutput, calls=%fused_computation.2 | convolution fusion | flops 3227512832 | bytes 12599296 | tf_op jit(solution)/shard_map/bkrd,bnkd->bkrn/dot_general | solution.py:36
  99.3 2.2 fusion.1
  101.6 15.4 %divide_bitcast_fusion = f32[2,128,2,8,128]{4,3,1,2,0:T(8,128)S(1)} fusion(f32[2,2,1024]{2,1,0:T(2,128)S(1)} %fusion.1, f32[2,2,512,2,128]{4,2,3,0,1:T(8,128)S(1)} %copy-done.5, f32[2,2,1024,512]{2,3,1,0:T(8,128)S(1)} %get-tuple-element.17, f32[2,2,1024]{2,1,0:T(2,128)S(1)} %broadcast_maximum_fusion, pred[2,1024,512]{1,2,0:T(8,128)(4,1)S(1)} %iota_compare_fusion), kind=kOutput, calls=%fused_computation.19 | convolution fusion | flops 3228041216 | bytes 12615680 | tf_op jit(solution)/shard_map/bkrn,bnkd->bkrd/dot_general | solution.py:21
  117.0 1.5 copy.153
  118.5 103.0 %all-reduce.2.cloned.1.call-done = f32[8,2,256,2,128]{4,2,3,0,1:T(8,128)} async-done(((f32[8,2,256,2,128]{4,2,3,0,1:T(8,128)}), f32[8,2,256,2,128]{4,2,3,0,1:T(8,128)}) %all-reduce.2.cloned.1.call-update) | async-done | bytes 4194320 | tf_op jit(solution)/shard_map/psum | solution.py:13
  221.5 4.1 %fusion.30 = (f32[8,2,64]{2,1,0:T(2,128)S(1)}, f32[8,2,64,256]{3,2,1,0:T(8,128)S(1)}) fusion(f32[8,2,64,128]{3,2,1,0:T(8,128)} %bitcast.142, f32[8,2,256,2,128]{4,2,3,0,1:T(8,128)} %all-reduce.2.cloned.1.call-done, pred[8,64,256]{2,1,0:T(8,128)(4,1)S(1)} %copy-done.6), kind=kOutput, calls=%fused_computation.70 | convolution fusion | flops 403438592 | bytes 3805184 | tf_op jit(solution)/shard_map/bkrd,bnkd->bkrn/dot_general | solution.py:36
  227.1 3.2 %all-to-all-start.2 = ((f32[2,1,512]{2,1,0:T(1,128)}), f32[2,1,512]{2,1,0:T(1,128)S(1)}, u32[]{:S(2)}, u32[]{:S(2)}) async-start(f32[2,1,512]{2,1,0:T(1,128)} %reshape.235), calls=%async_computation.2 | async-start | bytes 8192 | tf_op jit(solution)/shard_map/all_to_all | solution.py:129
  231.2 2.8 %all-to-all-done.2 = f32[2,1,512]{2,1,0:T(1,128)S(1)} async-done(((f32[2,1,512]{2,1,0:T(1,128)}), f32[2,1,512]{2,1,0:T(1,128)S(1)}, u32[]{:S(2)}, u32[]{:S(2)}) %all-to-all-start.2) | async-done | bytes 4128 | tf_op jit(solution)/shard_map/all_to_all | solution.py:129
  234.1 3.2 %all-to-all-start.1 = ((f32[2,1,512]{2,1,0:T(1,128)}), f32[2,1,512]{2,1,0:T(1,128)S(1)}, u32[]{:S(2)}, u32[]{:S(2)}) async-start(f32[2,1,512]{2,1,0:T(1,128)} %reshape.233), calls=%async_computation.1 | async-start | bytes 8192 | tf_op jit(solution)/shard_map/all_to_all | solution.py:128
  237.3 3.3 %fusion.7 = f32[8,2,64,128]{3,2,1,0:T(8,128)S(1)} fusion(f32[8,2,256,2,128]{4,2,3,0,1:T(8,128)} %all-reduce.2.cloned.1.call-done, f32[8,2,64,256]{3,2,1,0:T(8,128)S(1)} %get-tuple-element.19, f32[8,2,64]{2,1,0:T(2,128)S(1)} %broadcast_maximum_fusion.1), kind=kOutput, calls=%fused_computation.12 | convolution fusion | flops 402915328 | bytes 3674112 | tf_op jit(solution)/shard_map/bkrn,bnkd->bkrd/dot_general | solution.py:21
  242.8 3.5 %all-to-all-start = ((f32[2,8,1,4,16,128]{5,4,3,1,2,0:T(8,128)}), f32[2,8,1,4,16,128]{5,4,3,1,2,0:T(8,128)S(1)}, u32[]{:S(2)}, u32[]{:S(2)}) async-start(f32[2,8,1,4,16,128]{5,4,3,1,2,0:T(8,128)} %bitcast.137), calls=%async_computation | async-start | bytes 1048576 | tf_op jit(solution)/shard_map/all_to_all | solution.py:130
  247.6 5.7 %all-to-all-done = f32[2,8,1,4,16,128]{5,4,3,1,2,0:T(8,128)S(1)} async-done(((f32[2,8,1,4,16,128]{5,4,3,1,2,0:T(8,128)}), f32[2,8,1,4,16,128]{5,4,3,1,2,0:T(8,128)S(1)}, u32[]{:S(2)}, u32[]{:S(2)}) %all-to-all-start) | async-done | bytes 524320 | tf_op jit(solution)/shard_map/all_to_all | solution.py:130
  253.5 1.4 fusion.16
  (80 shorter events, 14.7 us)
Async XLA Ops:
  8.0 81.6 %copy-start = (f32[2,128,16,128]{3,2,1,0:T(8,128)S(1)}, f32[2,128,16,128]{3,2,1,0:T(8,128)}, u32[]{:S(2)}) copy-start(f32[2,128,16,128]{3,2,1,0:T(8,128)} %param.7) | copy-start | bytes 6291460
  8.0 51.4 %copy-start.1 = (f32[2,2,256,2,128]{4,3,2,1,0:T(2,128)S(1)}, f32[2,2,256,2,128]{4,3,2,1,0:T(2,128)}, u32[]{:S(2)}) copy-start(f32[2,2,256,2,128]{4,3,2,1,0:T(2,128)} %param.6) | copy-start | bytes 3145732
  8.0 81.5 %all-gather.3.cloned.1.call-start = ((), (), s32[]{:S(2)}) async-start(), calls=%async_computation.3 | async-start | bytes 3145728 | tf_op jit(solution)/shard_map/all_gather | solution.py:84
  10.5 15.1 %collective-permute-start = (f32[2,2,256,2,128]{4,2,3,0,1:T(8,128)}, f32[2,2,256,2,128]{4,2,3,0,1:T(8,128)S(1)}, u32[]{:S(2)}, u32[]{:S(2)}) collective-permute-start(f32[2,2,256,2,128]{4,2,3,0,1:T(8,128)} %copy.90), channel_id=1, source_target_pairs={{0,4},{4,8},{8,12},{12,0},{1,5},{5,9},{9,13},{13,1},{2,6},{6,10},{... | collective-permute-start | bytes 3145736 | tf_op jit(solution)/shard_map/ppermute | solution.py:98
  25.6 1.0 copy-start.2
  26.6 14.3 %collective-permute-start.1 = (f32[2,2,256,2,128]{4,2,3,0,1:T(8,128)S(1)}, f32[2,2,256,2,128]{4,2,3,0,1:T(8,128)}, u32[]{:S(2)}, u32[]{:S(2)}) collective-permute-start(f32[2,2,256,2,128]{4,2,3,0,1:T(8,128)S(1)} %collective-permute-done), channel_id=1, source_target_pairs={{0,4},{4,8},{8,12},{12,0},{1,5},{5,9},{9,13},{13,1},{2,6},{6,10},{... | collective-permute-start | bytes 3145736 | tf_op jit(solution)/shard_map/ppermute | solution.py:98
  40.9 14.5 %collective-permute-start.2 = (f32[2,2,256,2,128]{4,2,3,0,1:T(8,128)}, f32[2,2,256,2,128]{4,2,3,0,1:T(8,128)}, u32[]{:S(2)}, u32[]{:S(2)}) collective-permute-start(f32[2,2,256,2,128]{4,2,3,0,1:T(8,128)} %collective-permute-done.1), channel_id=1, source_target_pairs={{0,4},{4,8},{8,12},{12,0},{1,5},{5,9},{9,13},{13,1},{2,6},{6,10},{... | collective-permute-start | bytes 3145736 | tf_op jit(solution)/shard_map/ppermute | solution.py:98
  41.0 180.5 %all-reduce.2.cloned.1.call-start = ((), (), s32[]{:S(2)}) async-start(), calls=%async_computation.4 | async-start | bytes 8388608 | tf_op jit(solution)/shard_map/psum | solution.py:13
  41.0 21.0 %copy-start.3 = (f32[2,2,256,2,128]{4,2,3,0,1:T(8,128)S(1)}, f32[2,2,256,2,128]{4,2,3,0,1:T(8,128)}, u32[]{:S(2)}) copy-start(f32[2,2,256,2,128]{4,2,3,0,1:T(8,128)} %copy-done.2) | copy-start | bytes 3145732
  62.1 2.5 copy-start.10
  62.1 7.2 %copy-start.4 = (f32[8,1,4,16,128]{4,3,2,1,0:T(8,128)S(1)}, f32[8,1,4,16,128]{4,3,2,1,0:T(8,128)}, u32[]{:S(2)}) copy-start(f32[8,1,4,16,128]{4,3,2,1,0:T(8,128)} %param.8) | copy-start | bytes 786436
  62.2 20.7 %copy-start.9 = (s32[8]{0:T(128)S(1)}, s32[8]{0:T(128)}, u32[]{:S(2)}) copy-start(s32[8]{0:T(128)} %param.10) | copy-start | bytes 100
  62.2 21.1 %copy-start.8 = (f32[8,1,4,2,2,128]{5,4,3,2,1,0:T(2,128)S(1)}, f32[8,1,4,2,2,128]{5,4,3,2,1,0:T(2,128)}, u32[]{:S(2)}) copy-start(f32[8,1,4,2,2,128]{5,4,3,2,1,0:T(2,128)} %param.9) | copy-start | bytes 196612
  89.6 12.0 %copy-start.5 = (f32[2,2,512,2,128]{4,2,3,0,1:T(8,128)S(1)}, f32[2,2,512,2,128]{4,2,3,0,1:T(8,128)}, u32[]{:S(2)}) copy-start(f32[2,2,512,2,128]{4,2,3,0,1:T(8,128)} %all-gather.3.cloned.1.call-done) | copy-start | bytes 6291460
  101.6 119.9 %copy-start.6 = (pred[8,64,256]{2,1,0:T(8,128)(4,1)S(1)}, pred[8,64,256]{2,1,0:T(8,128)(4,1)}, u32[]{:S(2)}) copy-start(pred[8,64,256]{2,1,0:T(8,128)(4,1)} %broadcast_compare_fusion) | copy-start | bytes 393220
  117.0 130.2 %copy-start.7 = (f32[8,4,2,8]{3,1,2,0:T(4,128)S(1)}, f32[8,4,2,8]{3,1,2,0:T(4,128)}, u32[]{:S(2)}) copy-start(f32[8,4,2,8]{3,1,2,0:T(4,128)} %get-tuple-element.20) | copy-start | bytes 6148
  227.1 7.0 %all-to-all-start.2 = ((f32[2,1,512]{2,1,0:T(1,128)}), f32[2,1,512]{2,1,0:T(1,128)S(1)}, u32[]{:S(2)}, u32[]{:S(2)}) async-start(f32[2,1,512]{2,1,0:T(1,128)} %reshape.235), calls=%async_computation.2 | async-start | bytes 8192 | tf_op jit(solution)/shard_map/all_to_all | solution.py:129
  234.1 8.8 %all-to-all-start.1 = ((f32[2,1,512]{2,1,0:T(1,128)}), f32[2,1,512]{2,1,0:T(1,128)S(1)}, u32[]{:S(2)}, u32[]{:S(2)}) async-start(f32[2,1,512]{2,1,0:T(1,128)} %reshape.233), calls=%async_computation.1 | async-start | bytes 8192 | tf_op jit(solution)/shard_map/all_to_all | solution.py:128
  242.8 10.5 %all-to-all-start = ((f32[2,8,1,4,16,128]{5,4,3,1,2,0:T(8,128)}), f32[2,8,1,4,16,128]{5,4,3,1,2,0:T(8,128)S(1)}, u32[]{:S(2)}, u32[]{:S(2)}) async-start(f32[2,8,1,4,16,128]{5,4,3,1,2,0:T(8,128)} %bitcast.137), calls=%async_computation | async-start | bytes 1048576 | tf_op jit(solution)/shard_map/all_to_all | solution.py:130
Sparse Core Ops, SparseCore 0:
  41.1 39.8 all-gather.2
Sparse Core Ops, SparseCore 1:
  64.7 156.8 all-reduce.1
